TPU v7x, 32 devices: a whole 2x2x4 slice. The times are simulated.
32 devices in a mesh: replica: 8 (over y, x, core), fsdp: 4 (over z).
Axes of the slice: x: 2, y: 2, z: 4, core: 2. Of those that a mesh axis runs over, the one named last changes fastest.
Arguments:
- inputs: bfloat16 [8, 1024, 8192], P('replica', 'fsdp'), may hold values from -6 to 6
- cotangent: bfloat16 [8, 1024, 512], P('replica', 'fsdp'), may hold values from -6 to 6
- weight: bfloat16 [8, 8192, 512], P('replica', 'fsdp'), may hold values from -0.0625 to 0.0625
- adam_first: bfloat16 [8, 8192, 512], P('replica', 'fsdp'), may hold values from -0.1875 to 0.1875
- adam_second: bfloat16 [8, 8192, 512], P('replica', 'fsdp'), may hold values from 0.00024414062 to 0.00390625
- outer_frag: bfloat16 [32, 8192], P('fsdp'), may hold values from -6 to 6
- local_frag: bfloat16 [8, 32, 8192], P('replica', 'fsdp'), may hold values from -6 to 6
- momentum: float32 [32, 8192], P('fsdp'), may hold values from -3 to 3
Outputs:
- input_grad: bfloat16 [8, 1024, 8192], P('replica', 'fsdp')
- new_weight: bfloat16 [8, 8192, 512], P('replica', 'fsdp')
- new_first: bfloat16 [8, 8192, 512], P('replica', 'fsdp')
- new_second: bfloat16 [8, 8192, 512], P('replica', 'fsdp')
- new_outer: float32 [32, 8192], P('fsdp')
- new_momentum: float32 [32, 8192], P('fsdp')
All inputs are finite; a program needn't handle non-finite values.
Results may differ from a plain program's by a relative error of at most 0.0035.
Values may be sent and summed in bfloat16 or wider, within the bound.
A program may use at most 128 MiB of HBM per device.

v0:
```python
import jax
import jax.numpy as jnp
from jax import lax
from jax.sharding import PartitionSpec as P

beta_first = 0.9
beta_second = 0.95
adam_rate = 0.0003
adam_eps = 1e-08
first_fix = 1.0 - 0.9**10
second_fix = 1.0 - 0.95**10
outer_rate = 0.7
nesterov_mu = 0.9


def adam_update(weight_rows, first_moment, second_moment, gradient):
    first = beta_first * first_moment.astype(jnp.float32) + (1.0 - beta_first) * gradient
    second = (
        beta_second * second_moment.astype(jnp.float32) + (1.0 - beta_second) * gradient * gradient
    )
    step_size = first / first_fix / (jnp.sqrt(second / second_fix) + adam_eps)
    updated = weight_rows.astype(jnp.float32) - adam_rate * step_size
    return (updated.astype(jnp.bfloat16), first.astype(jnp.bfloat16), second.astype(jnp.bfloat16))


def on_device(inputs, cotangent, weight, adam_first, adam_second, outer_frag, local_frag, momentum):
    activations = inputs[0]
    cotangent_rows = cotangent[0]
    weight_rows = weight[0]
    groups = lax.axis_size("fsdp")
    tok_local = activations.shape[0]
    tok_replica = tok_local * groups
    input_grad = jnp.einsum(
        "tk,rk->tr",
        cotangent_rows,
        lax.all_gather(weight_rows, "fsdp", axis=0, tiled=True),
        preferred_element_type=jnp.float32,
    ).astype(jnp.bfloat16)
    summed = lax.psum_scatter(
        jnp.einsum(
            "td,tk->dk", activations, cotangent_rows, preferred_element_type=jnp.float32
        ).astype(jnp.bfloat16),
        "fsdp",
        scatter_dimension=0,
        tiled=True,
    ).astype(jnp.float32)
    gradient = summed / tok_replica
    updated, first, second = adam_update(weight_rows, adam_first[0], adam_second[0], gradient)
    replicas = lax.axis_size("replica")
    outer_wide = outer_frag.astype(jnp.float32)
    delta_local = outer_wide - local_frag[0].astype(jnp.float32)
    delta = lax.psum(delta_local, "replica") / replicas
    new_momentum = nesterov_mu * momentum + delta
    new_outer = outer_wide - outer_rate * (delta + nesterov_mu * new_momentum)
    return (input_grad[None], updated[None], first[None], second[None], new_outer, new_momentum)


def solution(mesh):
    return jax.shard_map(
        on_device,
        mesh=mesh,
        in_specs=(
            P("replica", "fsdp", None),
            P("replica", "fsdp", None),
            P("replica", "fsdp", None),
            P("replica", "fsdp", None),
            P("replica", "fsdp", None),
            P("fsdp", None),
            P("replica", "fsdp", None),
            P("fsdp", None),
        ),
        out_specs=(
            P("replica", "fsdp", None),
            P("replica", "fsdp", None),
            P("replica", "fsdp", None),
            P("replica", "fsdp", None),
            P("fsdp", None),
            P("fsdp", None),
        ),
        check_vma=False,
    )
```

profile of v0, /device:TPU:0, one launch (start us, length us, event | category | flops | bytes accessed | tf_op | source)
XLA Modules:
  0.0 324.8 jit_solution(11371701828479089676)
XLA Ops:
  8.0 0.0 copy-start
  8.0 0.0 all-reduce.2.cloned.1.call-start
  8.1 1.7 convert_subtract_fusion.2
  9.8 0.0 all-reduce.2.cloned.1.call-update
  9.8 0.0 all-gather.3.cloned.1.call-start
  9.9 0.5 all-gather.3.cloned.1.call-update
  10.4 0.0 reduce-scatter.2.cloned.1.call-start
  10.4 0.0 copy-done
  10.5 7.8 %convolution_convert_fusion = bf16[8192,512]{1,0:T(8,128)(2,1)} fusion(bf16[1,256,8192]{2,1,0:T(8,128)(2,1)} %param.8, bf16[1,256,512]{2,1,0:T(8,128)(2,1)S(1)} %copy-done), kind=kOutput, calls=%fused_computation | convolution fusion | flops 2151677952 | bytes 12845056 | tf_op jit(solution)/shard_map/td,tk->dk/dot_general | solution.py:40
  18.3 0.0 copy-start.2
  18.3 0.0 copy-start.3
  18.3 0.0 reduce-scatter.2.cloned.1.call-update
  18.3 50.4 %all-reduce.2.cloned.1.call-done = f32[8,8192]{1,0:T(8,128)} async-done(((f32[8,8192]{1,0:T(8,128)}), f32[8,8192]{1,0:T(8,128)}) %all-reduce.2.cloned.1.call-update) | async-done | bytes 262160 | tf_op jit(solution)/shard_map/psum | solution.py:52
  68.7 0.0 copy-done.2
  68.7 0.0 copy-done.3
  68.7 1.8 convert_subtract_fusion.1
  70.5 0.0 copy-start.1
  70.5 93.5 %all-gather.3.cloned.1.call-done = bf16[1,8192,512]{2,1,0:T(8,128)(2,1)} async-done(((bf16[1,2048,512]{2,1,0:T(8,128)(2,1)}), bf16[1,8192,512]{2,1,0:T(8,128)(2,1)}) %all-gather.3.cloned.1.call-update) | async-done | bytes 8388624 | tf_op jit(solution)/shard_map/all_gather | solution.py:36
  164.1 7.8 %fusion = bf16[1,256,8192]{2,1,0:T(8,128)(2,1)} fusion(bf16[1,8192,512]{2,1,0:T(8,128)(2,1)} %all-gather.3.cloned.1.call-done, bf16[1,256,512]{2,1,0:T(8,128)(2,1)S(1)} %copy-done), kind=kOutput, calls=%fused_computation.2 | convolution fusion | flops 2149580800 | bytes 12845056 | tf_op jit(solution)/shard_map/tk,rk->tr/dot_general | solution.py:33
  171.9 137.2 %reduce-scatter.2.cloned.1.call-done = bf16[2048,512]{1,0:T(8,128)(2,1)} async-done(((bf16[8192,512]{1,0:T(8,128)(2,1)}), bf16[2048,512]{1,0:T(8,128)(2,1)}) %reduce-scatter.2.cloned.1.call-update) | async-done | bytes 2097168 | tf_op jit(solution)/shard_map/reduce_scatter | solution.py:39
  309.0 0.0 copy-done.1
  309.0 8.4 %fusion.9 = (bf16[1,2048,512]{2,1,0:T(8,128)(2,1)}, bf16[1,2048,512]{2,1,0:T(8,128)(2,1)}, bf16[1,2048,512]{2,1,0:T(8,128)(2,1)}) fusion(bf16[2048,512]{1,0:T(8,128)(2,1)} %reduce-scatter.2.cloned.1.call-done, bf16[1,2048,512]{2,1,0:T(8,128)(2,1)} %param.12, bf16[1,2048,512]{2,1,0:T(8,128)(2,1)} %param.11, bf16[1,2048,512]{2,1,0:T(8,128)(2,1)S(1)} %copy-done.1), kind=kLoop, calls=%fused_computation.15 | loop fusion | flops 22020096 | bytes 14680064 | tf_op jit(solution)/shard_map/broadcast_in_dim | solution.py:55
Async XLA Ops:
  8.0 2.4 copy-start
  8.0 60.7 %all-reduce.2.cloned.1.call-start = ((), (), s32[]{:S(2)}) async-start(), calls=%async_computation.2 | async-start | bytes 524288 | tf_op jit(solution)/shard_map/psum | solution.py:52
  9.8 154.2 %all-gather.3.cloned.1.call-start = ((), (), s32[]{:S(2)}) async-start(), calls=%async_computation.3 | async-start | bytes 10485760 | tf_op jit(solution)/shard_map/all_gather | solution.py:36
  10.4 298.6 %reduce-scatter.2.cloned.1.call-start = ((), (), s32[]{:S(2)}) async-start(), calls=%async_computation.1 | async-start | bytes 10485760 | tf_op jit(solution)/shard_map/reduce_scatter | solution.py:39
  18.3 50.5 %copy-start.2 = (bf16[8,8192]{1,0:T(8,128)(2,1)S(1)}, bf16[8,8192]{1,0:T(8,128)(2,1)}, u32[]{:S(2)}) copy-start(bf16[8,8192]{1,0:T(8,128)(2,1)} %param.13) | copy-start | bytes 393220
  18.3 50.5 %copy-start.3 = (f32[8,8192]{1,0:T(8,128)S(1)}, f32[8,8192]{1,0:T(8,128)}, u32[]{:S(2)}) copy-start(f32[8,8192]{1,0:T(8,128)} %param.15) | copy-start | bytes 786436
  70.5 238.5 %copy-start.1 = (bf16[1,2048,512]{2,1,0:T(8,128)(2,1)S(1)}, bf16[1,2048,512]{2,1,0:T(8,128)(2,1)}, u32[]{:S(2)}) copy-start(bf16[1,2048,512]{2,1,0:T(8,128)(2,1)} %param.10) | copy-start | bytes 6291460
Sparse Core Ops, SparseCore 0:
  12.5 56.1 all-reduce.1
Sparse Core Ops, SparseCore 1:
  11.9 152.1 all-gather.2
  166.3 142.7 reduce-scatter.1
where the time goes:
time: 325 us
  waiting for transfers between devices  282 us (87%)
  matrix products  15.6 us (5%)
  between operations  15.5 us (5%)
  other arithmetic  11.9 us (4%)
    reduce_scatter x1, waiting for transfers between devices, on_device(): lax.psum_scatter(jnp.einsum('td,tk->dk', activations, cotangent_rows, pre...  137 us
    all_gather x1, waiting for transfers between devices, on_device(): lax.all_gather(weight_rows, 'fsdp', axis=0, tiled=True)  93.5 us
    psum x1, waiting for transfers between devices, on_device(): delta = lax.psum(delta_local, 'replica') / replicas  50.4 us
    broadcast_in_dim x1, other arithmetic, on_device(): second[None]  8.38 us
    dot_general x1, matrix products, on_device(): jnp.einsum('td,tk->dk', activations, cotangent_rows, preferred_element_ty...  7.81 us
    dot_general x1, matrix products, on_device(): jnp.einsum('tk,rk->tr', cotangent_rows, lax.all_gather(weight_rows, 'fsdp...  7.79 us
  transfers between devices with their start and end apart: 3, of which 3 were waited for; matrix products, arithmetic and copies ran while one was open for 5% of the time, Pallas kernels for 0%

commit v1 on v0

v1 whole, which is shorter than its diff:
```python
import functools

import jax
import jax.numpy as jnp
from jax import lax
from jax.experimental import pallas as pl
from jax.experimental.pallas import tpu as pltpu
from jax.sharding import PartitionSpec as P

beta_first = 0.9
beta_second = 0.95
adam_rate = 0.0003
adam_eps = 1e-08
first_fix = 1.0 - 0.9**10
second_fix = 1.0 - 0.95**10
outer_rate = 0.7
nesterov_mu = 0.9

MESH = pl.DeviceIdType.MESH
CHUNK = 256
WINDOW = 3
SUB = 32


def kernel(
    n,
    replicas,
    x_in,
    cot_in,
    w_in,
    m_in,
    v_in,
    outer_in,
    local_in,
    mom_in,
    out_o,
    w_o,
    m_o,
    v_o,
    outer_o,
    mom_o,
    x,
    cot,
    w,
    m,
    v,
    out,
    own,
    held,
    frag,
    outer,
    mom,
    new_outer,
    new_mom,
    load_sem,
    out_sem,
    new_sem,
    frag_out_sem,
    send_sem,
    recv_sem,
    frag_send,
    frag_recv,
):
    me = lax.axis_index("fsdp")
    rep = lax.axis_index("replica")
    rows = w.shape[0]
    chunk = min(CHUNK, rows)
    per = rows // chunk
    tokens = cot.shape[0] * n
    last = n - 1

    loads = [
        pltpu.make_async_copy(src, dst, load_sem.at[k])
        for k, (src, dst) in enumerate(
            [
                (cot_in, cot),
                (w_in, w),
                (x_in, x),
                (outer_in, outer),
                (mom_in, mom),
                (m_in, m),
                (v_in, v),
                (local_in, frag.at[rep]),
            ]
        )
    ]
    for load in loads:
        load.start()

    place = (me, last - me)
    ahead = (jnp.minimum(me + 1, last), jnp.maximum(me - 1, 0))

    barrier = pltpu.get_barrier_semaphore()
    for d in range(2):

        @pl.when(place[d] < last)
        def _():
            pl.semaphore_signal(barrier, inc=1, device_id={"fsdp": ahead[d]}, device_id_type=MESH)

    @pl.loop(1, replicas)
    def _(k):
        peer = lax.rem(rep + k, replicas)
        pl.semaphore_signal(barrier, inc=1, device_id={"replica": peer}, device_id_type=MESH)

    neighbours = jnp.where(me > 0, 1, 0) + jnp.where(me < last, 1, 0)
    pl.semaphore_wait(barrier, replicas - 1 + neighbours)

    def part_rows(c):
        return pl.ds(pl.multiple_of(c * chunk, chunk), chunk)

    def hop(d, t, c, src):
        return pltpu.make_async_remote_copy(
            src_ref=src,
            dst_ref=held.at[d, t, part_rows(c)],
            send_sem=send_sem.at[d, t * per + c],
            recv_sem=recv_sem.at[d, t * per + c],
            device_id={"fsdp": ahead[d]},
            device_id_type=MESH,
        )

    def wait_sent(d, s):
        t, c = s // per, lax.rem(s, per)
        hop(d, t, c, held.at[d, t, part_rows(c)]).wait_send()

    def wait_got(d, t, c):
        hop(d, t, c, held.at[d, t, part_rows(c)]).wait_recv()

    def frag_copy(k, owner):
        return pltpu.make_async_remote_copy(
            src_ref=frag.at[owner],
            dst_ref=frag.at[owner],
            send_sem=frag_send.at[k],
            recv_sem=frag_recv.at[owner],
            device_id={"replica": lax.rem(rep + k, replicas)},
            device_id_type=MESH,
        )

    def columns(owner, c):
        return pl.ds(pl.multiple_of(owner * rows + c * chunk, chunk), chunk)

    def grad_term(owner, c):
        return lax.dot_general(
            x[:, columns(owner, c)],
            cot[...],
            (((0,), (0,)), ((), ())),
            preferred_element_type=jnp.float32,
        )

    def out_copy(owner, c):
        return pltpu.make_async_copy(
            out.at[:, columns(owner, c)], out_o.at[:, columns(owner, c)], out_sem.at[owner, c]
        )

    def out_block(owner, c, block):
        out[:, columns(owner, c)] = lax.dot_general(
            cot[...], block, (((1,), (1,)), ((), ())), preferred_element_type=jnp.float32
        ).astype(out.dtype)
        out_copy(owner, c).start()

    def window(d, s):
        @pl.when(s >= WINDOW)
        def _():
            wait_sent(d, s - WINDOW)

    @pl.loop(0, per)
    def _(c):
        for d in range(2):

            @pl.when(place[d] < last)
            def _():
                window(d, c)
                hop(d, 0, c, w_in.at[part_rows(c)]).start()

        @pl.when(c == 0)
        def _():
            loads[7].wait()

            @pl.loop(1, replicas)
            def _(k):
                frag_copy(k, rep).start()

            for k in range(3):
                loads[k].wait()

        out_block(me, c, w[part_rows(c), :])
        own[part_rows(c), :] = grad_term(me, c)

    loads[3].wait()
    loads[4].wait()

    @pl.loop(1, replicas)
    def _(k):
        frag_copy(k, rep).wait_send()
        frag_copy(k, lax.rem(rep + k, replicas)).wait_recv()

    width = 1024

    @pl.loop(0, outer.shape[1] // width)
    def _(b):
        at = pl.ds(pl.multiple_of(b * width, width), width)
        wide = outer[:, at].astype(jnp.float32)
        total = jnp.zeros_like(wide)
        for q in range(replicas):
            total += wide - frag[q, :, at].astype(jnp.float32)
        delta = total / replicas
        momentum = nesterov_mu * mom[:, at] + delta
        new_mom[:, at] = momentum
        new_outer[:, at] = wide - outer_rate * (delta + nesterov_mu * momentum)

    frag_outs = [
        pltpu.make_async_copy(new_outer, outer_o, frag_out_sem.at[0]),
        pltpu.make_async_copy(new_mom, mom_o, frag_out_sem.at[1]),
    ]
    for copy in frag_outs:
        copy.start()

    @pl.loop(per, n * per)
    def _(s):
        t, c = s // per, lax.rem(s, per)
        for d in range(2):
            slot = held.at[d, t - 1, part_rows(c)]
            is_weight = t <= place[d]

            @pl.when(place[d] > 0)
            def _():
                wait_got(d, t - 1, c)

            @pl.when(jnp.logical_not(is_weight))
            def _():
                target = n + me - t if d == 0 else t + me - n
                term = grad_term(target, c)

                @pl.when(place[d] > 0)
                def _():
                    slot[...] = (slot[...].astype(jnp.float32) + term).astype(slot.dtype)

                @pl.when(place[d] == 0)
                def _():
                    slot[...] = term.astype(slot.dtype)

            @pl.when(place[d] < last)
            def _():
                window(d, s)
                hop(d, t, c, slot).start()

            @pl.when(is_weight)
            def _():
                out_block(me - t if d == 0 else me + t, c, slot[...])

    loads[5].wait()
    loads[6].wait()

    def new_copies(c):
        return [
            pltpu.make_async_copy(src.at[part_rows(c)], dst.at[part_rows(c)], new_sem.at[k, c])
            for k, (src, dst) in enumerate([(w, w_o), (m, m_o), (v, v_o)])
        ]

    @pl.loop(0, per)
    def _(c):
        for d in range(2):

            @pl.when(place[d] > 0)
            def _():
                wait_got(d, last, c)
                own[part_rows(c), :] += held[d, last, part_rows(c), :].astype(jnp.float32)

        @pl.loop(0, chunk // SUB)
        def _(b):
            at = pl.ds(pl.multiple_of(c * chunk + b * SUB, SUB), SUB)
            gradient = own[at, :] / tokens
            first = beta_first * m[at, :].astype(jnp.float32) + (1.0 - beta_first) * gradient
            second = (
                beta_second * v[at, :].astype(jnp.float32)
                + (1.0 - beta_second) * gradient * gradient
            )
            step_size = first / first_fix / (jnp.sqrt(second / second_fix) + adam_eps)
            w[at, :] = (w[at, :].astype(jnp.float32) - adam_rate * step_size).astype(w.dtype)
            m[at, :] = first.astype(m.dtype)
            v[at, :] = second.astype(v.dtype)

        for copy in new_copies(c):
            copy.start()

    for d in range(2):

        @pl.when(place[d] < last)
        def _():
            @pl.loop(n * per - WINDOW, n * per)
            def _(s):
                wait_sent(d, s)

    @pl.loop(0, n * per)
    def _(s):
        out_copy(s // per, lax.rem(s, per)).wait()

    for copy in frag_outs:
        copy.wait()

    @pl.loop(0, per)
    def _(c):
        for copy in new_copies(c):
            copy.wait()


def on_device(inputs, cotangent, weight, adam_first, adam_second, outer_frag, local_frag, momentum):
    n = lax.axis_size("fsdp")
    replicas = lax.axis_size("replica")
    x, cot, w, m, v, local = (
        inputs[0],
        cotangent[0],
        weight[0],
        adam_first[0],
        adam_second[0],
        local_frag[0],
    )
    rows, features = w.shape
    tokens, model = x.shape
    per = rows // min(CHUNK, rows)
    bf16, f32 = jnp.bfloat16, jnp.float32
    shape = jax.ShapeDtypeStruct
    anywhere = pl.BlockSpec(memory_space=pl.ANY)
    dma = pltpu.SemaphoreType.DMA
    results = pl.pallas_call(
        functools.partial(kernel, n, replicas),
        out_shape=(
            shape((tokens, model), bf16),
            shape(w.shape, bf16),
            shape(w.shape, bf16),
            shape(w.shape, bf16),
            shape(momentum.shape, f32),
            shape(momentum.shape, f32),
        ),
        in_specs=[anywhere] * 8,
        out_specs=[anywhere] * 6,
        scratch_shapes=[
            pltpu.VMEM((tokens, model), bf16),
            pltpu.VMEM((tokens, features), bf16),
            pltpu.VMEM(w.shape, bf16),
            pltpu.VMEM(w.shape, bf16),
            pltpu.VMEM(w.shape, bf16),
            pltpu.VMEM((tokens, model), bf16),
            pltpu.VMEM(w.shape, f32),
            pltpu.VMEM((2, n, rows, features), bf16),
            pltpu.VMEM((replicas,) + local.shape, bf16),
            pltpu.VMEM(outer_frag.shape, bf16),
            pltpu.VMEM(momentum.shape, f32),
            pltpu.VMEM(momentum.shape, f32),
            pltpu.VMEM(momentum.shape, f32),
            dma((8,)),
            dma((n, per)),
            dma((3, per)),
            dma((2,)),
            dma((2, n * per)),
            dma((2, n * per)),
            dma((replicas,)),
            dma((replicas,)),
        ],
        compiler_params=pltpu.CompilerParams(
            collective_id=0, has_side_effects=True, vmem_limit_bytes=48 * 1024 * 1024
        ),
        cost_estimate=pl.CostEstimate(
            flops=4 * tokens * model * features,
            bytes_accessed=4 * tokens * model + 12 * rows * features,
            transcendentals=rows * features,
        ),
    )(x, cot, w, m, v, outer_frag, local, momentum)
    input_grad, updated, first, second, new_outer, new_momentum = results
    return (input_grad[None], updated[None], first[None], second[None], new_outer, new_momentum)


def solution(mesh):
    return jax.shard_map(
        on_device,
        mesh=mesh,
        in_specs=(
            P("replica", "fsdp", None),
            P("replica", "fsdp", None),
            P("replica", "fsdp", None),
            P("replica", "fsdp", None),
            P("replica", "fsdp", None),
            P("fsdp", None),
            P("replica", "fsdp", None),
            P("fsdp", None),
        ),
        out_specs=(
            P("replica", "fsdp", None),
            P("replica", "fsdp", None),
            P("replica", "fsdp", None),
            P("replica", "fsdp", None),
            P("fsdp", None),
            P("fsdp", None),
        ),
        check_vma=False,
    )
```

time: 325 us -> 206 us (0.63)
  waiting for transfers between devices: 282 us -> 0 us
  Pallas kernels: 0 us -> 190 us
  matrix products: 15.6 us -> 0 us
  between operations: 15.5 us -> 0.66 us
  local copies, waits for them, and re-layouts: 0.02 us -> 14.7 us
  other arithmetic: 11.9 us -> 0 us
    pallas_call x0 -> x1, Pallas kernels: none -> 190 us  [on_device(): pl.pallas_call(functools.partial(kernel, n, replicas), out_shape=(shape((...]
    reduce_scatter x1 -> x0, waiting for transfers between devices: 137 us -> none  [on_device(): lax.psum_scatter(jnp.einsum('td,tk->dk', activations, cotangent_rows, pre...]
    all_gather x1 -> x0, waiting for transfers between devices: 93.5 us -> none  [on_device(): lax.all_gather(weight_rows, 'fsdp', axis=0, tiled=True)]
    psum x1 -> x0, waiting for transfers between devices: 50.4 us -> none  [on_device(): delta = lax.psum(delta_local, 'replica') / replicas]
    dot_general x2 -> x0, matrix products: 15.6 us -> none  [the longest x1 7.81 us: on_device(): jnp.einsum('td,tk->dk', activations, cotangent_rows, preferred_element_ty...]
    unnamed x8 -> x16, local copies, waits for them, and re-layouts: 0.02 us -> 14.7 us
    broadcast_in_dim x1 -> x0, other arithmetic: 8.38 us -> none  [on_device(): second[None]]
    sub x2 -> x0, other arithmetic: 3.54 us -> none  [the longest x1 1.81 us: on_device(): new_outer = outer_wide - outer_rate * (delta + nesterov_mu * new_momentum)]
  transfers between devices with their start and end apart: 3 -> 0, of which waited for: 3 -> 0; matrix products, arithmetic and copies ran while one was open for 5% -> 0% of each run, Pallas kernels for 0% -> 0%
where the time goes in v1:
time: 206 us; the launch traced here: 205 us
  Pallas kernels  190 us (92%)
  local copies, waits for them, and re-layouts  14.7 us (7%)
    pallas_call x1, Pallas kernels, on_device(): pl.pallas_call(functools.partial(kernel, n, replicas), out_shape=(shape((...  190 us
    unnamed x16, local copies, waits for them, and re-layouts  14.7 us

profile of v1, /device:TPU:0, one launch (start us, length us, event | category | flops | bytes accessed | tf_op | source)
XLA Modules:
  0.0 205.5 jit_solution(18370471758641768842)
XLA Ops:
  0.6 0.0 copy-start
  0.6 0.9 copy-done
  1.6 0.0 copy-start.1
  1.6 0.9 copy-done.1
  2.5 0.0 copy-start.2
  2.5 0.9 copy-done.2
  3.4 0.0 copy-start.3
  3.4 0.9 copy-done.3
  4.3 190.1 %shard_map.127 = (bf16[256,8192]{1,0:T(8,128)(2,1)}, bf16[2048,512]{1,0:T(8,128)(2,1)S(1)}, bf16[2048,512]{1,0:T(8,128)(2,1)S(1)}, bf16[2048,512]{1,0:T(8,128)(2...) custom-call(bf16[256,8192]{1,0:T(8,128)(2,1)} %bitcast.16, bf16[256,512]{1,0:T(8,128)(2,1)S(1)} %bitcast.12, ...), custom_call_target="tpu_custom_call" | custom-call | flops 4294967296 | bytes 20971520 | tf_op jit(solution)/shard_map/pallas_call | solution.py:324
  194.5 4.6 %copy.20 = bf16[1,256,8192]{2,1,0:T(8,128)(2,1)} copy(bf16[1,256,8192]{2,1,0:T(8,128)(2,1)} %bitcast.14) | data formatting | bytes 8388608
  199.1 1.3 copy.21
  200.4 0.0 copy-start.4
  200.4 1.3 copy.22
  201.7 1.0 copy-done.4
  202.8 1.3 copy.23
  204.1 0.7 copy.24
  204.8 0.7 copy.25
Async XLA Ops:
  0.6 1.0 copy-start
  1.6 0.9 copy-start.1
  2.5 0.9 copy-start.2
  3.4 0.9 copy-start.3
  200.4 2.3 %copy-start.4 = (bf16[2048,512]{1,0:T(8,128)(2,1)S(1)}, bf16[2048,512]{1,0:T(8,128)(2,1)}, u32[]{:S(2)}) copy-start(bf16[2048,512]{1,0:T(8,128)(2,1)} %get-tuple-element.15) | copy-start | bytes 6291460

commit v2 on v1

--- a/solution.py
+++ b/solution.py
@@ -33,29 +33,20 @@
     outer_in,
     local_in,
     mom_in,
-    out_o,
-    w_o,
-    m_o,
-    v_o,
-    outer_o,
-    mom_o,
-    x,
-    cot,
+    out,
     w,
     m,
     v,
-    out,
+    new_outer,
+    new_mom,
+    x,
+    cot,
     own,
     held,
     frag,
     outer,
     mom,
-    new_outer,
-    new_mom,
     load_sem,
-    out_sem,
-    new_sem,
-    frag_out_sem,
     send_sem,
     recv_sem,
     frag_send,
@@ -146,16 +137,10 @@
             preferred_element_type=jnp.float32,
         )
 
-    def out_copy(owner, c):
-        return pltpu.make_async_copy(
-            out.at[:, columns(owner, c)], out_o.at[:, columns(owner, c)], out_sem.at[owner, c]
-        )
-
     def out_block(owner, c, block):
         out[:, columns(owner, c)] = lax.dot_general(
             cot[...], block, (((1,), (1,)), ((), ())), preferred_element_type=jnp.float32
         ).astype(out.dtype)
-        out_copy(owner, c).start()
 
     def window(d, s):
         @pl.when(s >= WINDOW)
@@ -207,13 +192,6 @@
         new_mom[:, at] = momentum
         new_outer[:, at] = wide - outer_rate * (delta + nesterov_mu * momentum)
 
-    frag_outs = [
-        pltpu.make_async_copy(new_outer, outer_o, frag_out_sem.at[0]),
-        pltpu.make_async_copy(new_mom, mom_o, frag_out_sem.at[1]),
-    ]
-    for copy in frag_outs:
-        copy.start()
-
     @pl.loop(per, n * per)
     def _(s):
         t, c = s // per, lax.rem(s, per)
@@ -249,12 +227,6 @@
 
     loads[5].wait()
     loads[6].wait()
-
-    def new_copies(c):
-        return [
-            pltpu.make_async_copy(src.at[part_rows(c)], dst.at[part_rows(c)], new_sem.at[k, c])
-            for k, (src, dst) in enumerate([(w, w_o), (m, m_o), (v, v_o)])
-        ]
 
     @pl.loop(0, per)
     def _(c):
@@ -279,9 +251,6 @@
             m[at, :] = first.astype(m.dtype)
             v[at, :] = second.astype(v.dtype)
 
-        for copy in new_copies(c):
-            copy.start()
-
     for d in range(2):
 
         @pl.when(place[d] < last)
@@ -290,17 +259,16 @@
             def _(s):
                 wait_sent(d, s)
 
-    @pl.loop(0, n * per)
-    def _(s):
-        out_copy(s // per, lax.rem(s, per)).wait()
-
-    for copy in frag_outs:
+
+def write_kernel(*refs):
+    count = (len(refs) - 1) // 2
+    copies = [
+        pltpu.make_async_copy(refs[k], refs[count + k], refs[-1].at[k]) for k in range(count)
+    ]
+    for copy in copies:
+        copy.start()
+    for copy in copies:
         copy.wait()
-
-    @pl.loop(0, per)
-    def _(c):
-        for copy in new_copies(c):
-            copy.wait()
 
 
 def on_device(inputs, cotangent, weight, adam_first, adam_second, outer_frag, local_frag, momentum):
@@ -319,52 +287,55 @@
     per = rows // min(CHUNK, rows)
     bf16, f32 = jnp.bfloat16, jnp.float32
     shape = jax.ShapeDtypeStruct
-    anywhere = pl.BlockSpec(memory_space=pl.ANY)
+    hbm, vmem = pl.BlockSpec(memory_space=pltpu.HBM), pl.BlockSpec(memory_space=pltpu.VMEM)
     dma = pltpu.SemaphoreType.DMA
+    kinds = [
+        ((tokens, model), bf16),
+        (w.shape, bf16),
+        (w.shape, bf16),
+        (w.shape, bf16),
+        (momentum.shape, f32),
+        (momentum.shape, f32),
+    ]
     results = pl.pallas_call(
         functools.partial(kernel, n, replicas),
-        out_shape=(
-            shape((tokens, model), bf16),
-            shape(w.shape, bf16),
-            shape(w.shape, bf16),
-            shape(w.shape, bf16),
-            shape(momentum.shape, f32),
-            shape(momentum.shape, f32),
-        ),
-        in_specs=[anywhere] * 8,
-        out_specs=[anywhere] * 6,
+        out_shape=[pltpu.VMEM(*kind) for kind in kinds],
+        in_specs=[hbm] * 8,
+        out_specs=[vmem] * 6,
         scratch_shapes=[
             pltpu.VMEM((tokens, model), bf16),
             pltpu.VMEM((tokens, features), bf16),
-            pltpu.VMEM(w.shape, bf16),
-            pltpu.VMEM(w.shape, bf16),
-            pltpu.VMEM(w.shape, bf16),
-            pltpu.VMEM((tokens, model), bf16),
             pltpu.VMEM(w.shape, f32),
             pltpu.VMEM((2, n, rows, features), bf16),
             pltpu.VMEM((replicas,) + local.shape, bf16),
             pltpu.VMEM(outer_frag.shape, bf16),
             pltpu.VMEM(momentum.shape, f32),
-            pltpu.VMEM(momentum.shape, f32),
-            pltpu.VMEM(momentum.shape, f32),
             dma((8,)),
-            dma((n, per)),
-            dma((3, per)),
-            dma((2,)),
             dma((2, n * per)),
             dma((2, n * per)),
             dma((replicas,)),
             dma((replicas,)),
         ],
         compiler_params=pltpu.CompilerParams(
-            collective_id=0, has_side_effects=True, vmem_limit_bytes=48 * 1024 * 1024
+            collective_id=0, has_side_effects=True, vmem_limit_bytes=40 * 1024 * 1024
         ),
         cost_estimate=pl.CostEstimate(
             flops=4 * tokens * model * features,
             bytes_accessed=4 * tokens * model + 12 * rows * features,
             transcendentals=rows * features,
         ),
-    )(x, cot, w, m, v, outer_frag, local, momentum)
+    )(*[
+        pltpu.with_memory_space_constraint(a, pltpu.HBM)
+        for a in (x, cot, w, m, v, outer_frag, local, momentum)
+    ])
+    results = pl.pallas_call(
+        write_kernel,
+        out_shape=[shape(*kind) for kind in kinds],
+        in_specs=[pl.BlockSpec(memory_space=pl.ANY)] * 6,
+        out_specs=[hbm] * 6,
+        scratch_shapes=[dma((6,))],
+        compiler_params=pltpu.CompilerParams(vmem_limit_bytes=1024 * 1024),
+    )(*[pltpu.with_memory_space_constraint(a, pltpu.VMEM) for a in results])
     input_grad, updated, first, second, new_outer, new_momentum = results
     return (input_grad[None], updated[None], first[None], second[None], new_outer, new_momentum)
 

time: 206 us -> 193 us (0.937)
  local copies, waits for them, and re-layouts: 14.7 us -> 0 us
  Pallas kernels: 190 us -> 193 us
    unnamed x16 -> x0, local copies, waits for them, and re-layouts: 14.7 us -> none
    pallas_call x1 -> x2, Pallas kernels: 190 us -> 193 us  [the longest x1 189 us: on_device(): pl.pallas_call(functools.partial(kernel, n, replicas), out_shape=[pltpu.V...]
where the time goes in v2:
time: 193 us
  Pallas kernels  193 us (100%)
    pallas_call x1, Pallas kernels, on_device(): pl.pallas_call(functools.partial(kernel, n, replicas), out_shape=[pltpu.V...  189 us
    pallas_call x1, Pallas kernels, on_device(): pl.pallas_call(write_kernel, out_shape=[shape(*kind) for kind in kinds],...  4.11 us

profile of v2, /device:TPU:0, one launch (start us, length us, event | category | flops | bytes accessed | tf_op | source)
XLA Modules:
  0.0 193.3 jit_solution(9436143689608747063)
XLA Ops:
  0.6 188.6 %shard_map.127 = (bf16[256,8192]{1,0:T(8,128)(2,1)S(1)}, bf16[2048,512]{1,0:T(8,128)(2,1)S(1)}, bf16[2048,512]{1,0:T(8,128)(2,1)S(1)}, bf16[2048,512]{1,0:T(8,12...) custom-call(bf16[256,8192]{1,0:T(8,128)(2,1)} %bitcast.10, bf16[256,512]{1,0:T(8,128)(2,1)} %bitcast.18, ...), custom_call_target="tpu_custom_call" | custom-call | flops 4294967296 | bytes 20971520 | tf_op jit(solution)/shard_map/pallas_call | solution.py:300
  189.2 4.1 %shard_map.128 = (bf16[256,8192]{1,0:T(8,128)(2,1)}, bf16[2048,512]{1,0:T(8,128)(2,1)}, bf16[2048,512]{1,0:T(8,128)(2,1)}, bf16[2048,512]{1,0:T(8,128)(2,1)}, f32[8,8192]{1,0:T(8,128)}, /*index=5*/f32[8,8192]{1,0:T(8,128)}) custom-call(bf16[256,8192]{1,0:T(8,128)(2,1)S(1)} %get-tuple-element.18.refs_0_, bf16[2048,512]{1,0:T(8,128)(2,1)S(1)} %get-tuple-element.19.refs_1_, ...), custom_call_target="tpu_custom_call" | custom-call | tf_op jit(solution)/shard_map/pallas_call | solution.py:331
